TPU v7x, 256 devices: a whole 4x4x8 slice. The times are simulated.
256 devices in a mesh: blk: 32 (over x_hi, z, core), grp: 8 (over y, x_lo).
Axes of the slice: x: 4 (x_hi: 2, x_lo: 2; x = x_hi * 2 + x_lo), y: 4, z: 8, core: 2. Of those that a mesh axis runs over, the one named last changes fastest.
Arguments:
- embedding: bfloat16 [262144, 512], P(('blk', 'grp')), may hold values from -2 to 2
- direction: float32 [262144, 32], P(('blk', 'grp'))
- residual: float32 [262144, 32], P(('blk', 'grp'))
- solution: float32 [262144, 32], P(('blk', 'grp')), may hold values from -6 to 6
- prior: float32 [262144, 32], P(('blk', 'grp')), may hold values from -6 to 6
- plan: int32 [255], replicated, may hold values from 1 to 255, as said below
- round_index: int32 [1], replicated, may hold values from 0 to 252
Outputs:
- new_solution: float32 [262144, 32], P(('blk', 'grp'))
- new_residual: float32 [262144, 32], P(('blk', 'grp'))
- new_direction: float32 [262144, 32], P(('blk', 'grp'))
Inputs may be any that keep to these rules, and one draw needn't show every extreme that they name: `plan`: every value 1 to 255 appears exactly once.
All inputs are finite; a program needn't handle non-finite values.
Results may differ from a plain program's by a relative error of at most 0.0049.
Values may be sent and summed in bfloat16 or wider, within the bound.
A program may use at most 64 MiB of HBM per device.

v0:
```python
import jax
import jax.numpy as jnp
from jax import lax
from jax.sharding import PartitionSpec as P

ROUNDS = 3


AMPLITUDE = 2.0
GAMMA = 2.0
NOISE = 1.0


def for_sending(shard):

    def short(part):
        return part.astype(jnp.bfloat16) if part.dtype == jnp.float32 else part

    return jax.tree.map(short, shard)


def from_partner(block, axis, apart):
    count = lax.axis_size(axis)
    route = []
    for low in range(count):
        high = low | 1 << apart
        if high != low and high < count:
            route += [(low, high), (high, low)]
    return lax.ppermute(block, axis, route)


def kernel_block(left, left_sq, right, right_sq):
    cross = lax.dot_general(
        left, right, (((1,), (1,)), ((), ())), preferred_element_type=jnp.float32
    )
    dist = left_sq[:, None] + right_sq[None, :] - 2.0 * cross
    return (AMPLITUDE * jnp.exp(-GAMMA * dist)).astype(jnp.bfloat16)


def staying(payload):
    return payload


def carry_along(points, point_dir, xor_mask, bit_list):
    for bit_number in bit_list:
        flagged = jnp.bitwise_and(jnp.right_shift(xor_mask, bit_number), 1) == 1

        def crossing(payload):
            arrived = jax.tree.map(
                lambda part, own: part.astype(own.dtype),
                from_partner(for_sending(payload), ("blk", "grp"), bit_number),
                payload,
            )
            return (arrived[0], arrived[1])

        points, point_dir = lax.cond(flagged, crossing, staying, (points, point_dir))
    return (points, point_dir)


def local(embedding, direction, residual, solution, prior, plan, round_index):
    total_bits = lax.axis_size(("blk", "grp")).bit_length() - 1
    bit_list = list(range(total_bits))
    num_rows = embedding.shape[0]
    num_probes = direction.shape[1]
    own_sq = jnp.sum(jnp.square(embedding.astype(jnp.float32)), axis=1)
    own_dir = direction.astype(jnp.bfloat16)
    rounds_sum = jnp.zeros((num_rows, num_probes), jnp.float32)
    for step in range(ROUNDS):
        xor_mask = lax.dynamic_index_in_dim(plan, round_index[0] + step, 0, keepdims=False)
        partner_x, partner_dir = carry_along(embedding, own_dir, xor_mask, bit_list)
        partner_sq = jnp.sum(jnp.square(partner_x.astype(jnp.float32)), axis=1)
        kern = kernel_block(embedding, own_sq, partner_x, partner_sq)
        rounds_sum = rounds_sum + jnp.dot(kern, partner_dir, preferred_element_type=jnp.float32)
    image = prior + rounds_sum + NOISE * direction
    local_norm = jnp.sum(residual * residual, axis=0)
    local_curv = jnp.sum(direction * image, axis=0)
    norm_now, curvature = lax.psum((local_norm, local_curv), ("blk", "grp"))
    alpha = norm_now / curvature
    new_solution = solution + alpha * direction
    new_residual = residual - alpha * image
    norm_next = lax.psum(jnp.sum(new_residual * new_residual, axis=0), ("blk", "grp"))
    new_direction = new_residual + norm_next / norm_now * direction
    return (new_solution, new_residual, new_direction)


def solution(mesh):
    in_specs = (
        P(("blk", "grp"), None),
        P(("blk", "grp"), None),
        P(("blk", "grp"), None),
        P(("blk", "grp"), None),
        P(("blk", "grp"), None),
        P(),
        P(),
    )
    out_specs = (P(("blk", "grp"), None), P(("blk", "grp"), None), P(("blk", "grp"), None))
    return jax.shard_map(local, mesh=mesh, in_specs=in_specs, out_specs=out_specs, check_vma=False)
```

profile of v0, /device:TPU:1, one launch (start us, length us, event | category | flops | bytes accessed | tf_op | source)
XLA Modules:
  0.0 597.1 jit_solution(7691470558218295436)
XLA Ops:
  20.3 29.5 %conditional.40 = (bf16[1024,512]{1,0:T(8,128)(2,1)}, bf16[1024,32]{1,0:T(8,128)(2,1)}) conditional(s32[]{:T(128)} %bitcast.26, (bf16[1024,512]{1,0:T(8,128)(2,1)}, bf16[1024,32]{1,0:T(8,128)(2,1)S(1)}) %tuple.134, (bf16[1024,512]{1,0:T(8,128)(2,1)}, bf16[1024,32]{1,0:T(8,128)(2,1)S(1)}) %tuple.134), branch_computations={%region_37.38_spmd, %region_38.39_spmd} | conditional | bytes 4456544 | solution.py:56
  22.6 27.3 %collective-permute-done.33 = bf16[1024,32]{1,0:T(8,128)(2,1)} collective-permute-done((bf16[1024,32]{1,0:T(8,128)(2,1)S(1)}, bf16[1024,32]{1,0:T(8,128)(2,1)}, u32[]{:S(2)}, u32[]{:S(2)}) %collective-permute-start.33) | collective-permute-done | bytes 65568 | tf_op jit(solution)/shard_map/cond/branch_1_fun/ppermute | solution.py:29
  49.8 32.0 %conditional.41 = ((bf16[1024,512]{1,0:T(8,128)(2,1)}, bf16[1024,32]{1,0:T(8,128)(2,1)})) conditional(s32[]{:T(128)} %bitcast.25, (bf16[1024,512]{1,0:T(8,128)(2,1)}, bf16[1024,32]{1,0:T(8,128)(2,1)}) %conditional.40, (bf16[1024,512]{1,0:T(8,128)(2,1)}, bf16[1024,32]{1,0:T(8,128)(2,1)}) %conditional.40), branch_computations={%region_39.40_spmd, %region_40.41_spmd} | conditional | bytes 6684776 | solution.py:56
  52.6 27.5 %collective-permute-done.35 = bf16[1024,32]{1,0:T(8,128)(2,1)S(1)} collective-permute-done((bf16[1024,32]{1,0:T(8,128)(2,1)}, bf16[1024,32]{1,0:T(8,128)(2,1)S(1)}, u32[]{:S(2)}, u32[]{:S(2)}) %collective-permute-start.35) | collective-permute-done | bytes 65568 | tf_op jit(solution)/shard_map/cond/branch_1_fun/ppermute | solution.py:29
  81.8 7.0 %conditional.43 = ((bf16[1024,512]{1,0:T(8,128)(2,1)}, bf16[1024,32]{1,0:T(8,128)(2,1)})) conditional(s32[]{:T(128)} %bitcast.23, (bf16[1024,512]{1,0:T(8,128)(2,1)}, bf16[1024,32]{1,0:T(8,128)(2,1)}) %get-tuple-element.379, (bf16[1024,512]{1,0:T(8,128)(2,1)}, bf16[1024,32]{1,0:T(8,128)(2,1)}) %get-tuple-element.379), branch_computations={%region_43.44_spmd, %region_44.45_spmd} | conditional | bytes 6684776 | solution.py:56
  88.8 32.6 %conditional.44 = ((bf16[1024,512]{1,0:T(8,128)(2,1)}, bf16[1024,32]{1,0:T(8,128)(2,1)})) conditional(s32[]{:T(128)} %bitcast.22, (bf16[1024,512]{1,0:T(8,128)(2,1)}, bf16[1024,32]{1,0:T(8,128)(2,1)}) %get-tuple-element.380, (bf16[1024,512]{1,0:T(8,128)(2,1)}, bf16[1024,32]{1,0:T(8,128)(2,1)}) %get-tuple-element.380), branch_computations={%region_45.46_spmd, %region_46.47_spmd} | conditional | bytes 6684776 | solution.py:56
  90.6 29.0 %collective-permute-done.41 = bf16[1024,32]{1,0:T(8,128)(2,1)S(1)} collective-permute-done((bf16[1024,32]{1,0:T(8,128)(2,1)}, bf16[1024,32]{1,0:T(8,128)(2,1)S(1)}, u32[]{:S(2)}, u32[]{:S(2)}) %collective-permute-start.41) | collective-permute-done | bytes 65568 | tf_op jit(solution)/shard_map/cond/branch_1_fun/ppermute | solution.py:29
  121.3 61.1 %conditional.45 = ((bf16[1024,512]{1,0:T(8,128)(2,1)}, bf16[1024,32]{1,0:T(8,128)(2,1)})) conditional(s32[]{:T(128)} %bitcast.21, (bf16[1024,512]{1,0:T(8,128)(2,1)}, bf16[1024,32]{1,0:T(8,128)(2,1)}) %get-tuple-element.381, (bf16[1024,512]{1,0:T(8,128)(2,1)}, bf16[1024,32]{1,0:T(8,128)(2,1)}) %get-tuple-element.381), branch_computations={%region_47.48_spmd, %region_48.49_spmd} | conditional | bytes 6684776 | solution.py:56
  124.2 56.5 %collective-permute-done.43 = bf16[1024,32]{1,0:T(8,128)(2,1)S(1)} collective-permute-done((bf16[1024,32]{1,0:T(8,128)(2,1)}, bf16[1024,32]{1,0:T(8,128)(2,1)S(1)}, u32[]{:S(2)}, u32[]{:S(2)}) %collective-permute-start.43) | collective-permute-done | bytes 65568 | tf_op jit(solution)/shard_map/cond/branch_1_fun/ppermute | solution.py:29
  182.4 32.2 %conditional.47 = ((bf16[1024,512]{1,0:T(8,128)(2,1)}, bf16[1024,32]{1,0:T(8,128)(2,1)})) conditional(s32[]{:T(128)} %bitcast.19, (bf16[1024,512]{1,0:T(8,128)(2,1)}, bf16[1024,32]{1,0:T(8,128)(2,1)}) %get-tuple-element.383, (bf16[1024,512]{1,0:T(8,128)(2,1)}, bf16[1024,32]{1,0:T(8,128)(2,1)}) %get-tuple-element.383), branch_computations={%region_51.52_spmd, %region_52.53_spmd} | conditional | bytes 6684776 | solution.py:56
  185.4 27.5 %collective-permute-done.47 = bf16[1024,32]{1,0:T(8,128)(2,1)S(1)} collective-permute-done((bf16[1024,32]{1,0:T(8,128)(2,1)}, bf16[1024,32]{1,0:T(8,128)(2,1)S(1)}, u32[]{:S(2)}, u32[]{:S(2)}) %collective-permute-start.47) | collective-permute-done | bytes 65568 | tf_op jit(solution)/shard_map/cond/branch_1_fun/ppermute | solution.py:29
  216.1 28.1 %conditional.32 = (bf16[1024,512]{1,0:T(8,128)(2,1)}, bf16[1024,32]{1,0:T(8,128)(2,1)}) conditional(s32[]{:T(128)} %bitcast.17, (bf16[1024,512]{1,0:T(8,128)(2,1)S(1)}, bf16[1024,32]{1,0:T(8,128)(2,1)S(1)}) %tuple.232, (bf16[1024,512]{1,0:T(8,128)(2,1)S(1)}, bf16[1024,32]{1,0:T(8,128)(2,1)S(1)}) %tuple.233), branch_computations={%region_20.21_spmd, %region_21.22_spmd} | conditional | bytes 4456544 | solution.py:56
  217.7 26.5 %collective-permute-done.17 = bf16[1024,32]{1,0:T(8,128)(2,1)} collective-permute-done((bf16[1024,32]{1,0:T(8,128)(2,1)S(1)}, bf16[1024,32]{1,0:T(8,128)(2,1)}, u32[]{:S(2)}, u32[]{:S(2)}) %collective-permute-start.17) | collective-permute-done | bytes 65568 | tf_op jit(solution)/shard_map/cond/branch_1_fun/ppermute | solution.py:29
  244.2 28.8 %conditional.33 = ((bf16[1024,512]{1,0:T(8,128)(2,1)}, bf16[1024,32]{1,0:T(8,128)(2,1)})) conditional(s32[]{:T(128)} %bitcast.16, (bf16[1024,512]{1,0:T(8,128)(2,1)}, bf16[1024,32]{1,0:T(8,128)(2,1)}) %conditional.32, (bf16[1024,512]{1,0:T(8,128)(2,1)}, bf16[1024,32]{1,0:T(8,128)(2,1)}) %conditional.32), branch_computations={%region_22.23_spmd, %region_23.24_spmd} | conditional | bytes 6684776 | solution.py:56
  245.7 25.7 %collective-permute-done.19 = bf16[1024,32]{1,0:T(8,128)(2,1)S(1)} collective-permute-done((bf16[1024,32]{1,0:T(8,128)(2,1)}, bf16[1024,32]{1,0:T(8,128)(2,1)S(1)}, u32[]{:S(2)}, u32[]{:S(2)}) %collective-permute-start.19) | collective-permute-done | bytes 65568 | tf_op jit(solution)/shard_map/cond/branch_1_fun/ppermute | solution.py:29
  273.0 8.8 %conditional.35 = ((bf16[1024,512]{1,0:T(8,128)(2,1)}, bf16[1024,32]{1,0:T(8,128)(2,1)})) conditional(s32[]{:T(128)} %bitcast.14, (bf16[1024,512]{1,0:T(8,128)(2,1)}, bf16[1024,32]{1,0:T(8,128)(2,1)}) %get-tuple-element.372, (bf16[1024,512]{1,0:T(8,128)(2,1)}, bf16[1024,32]{1,0:T(8,128)(2,1)}) %get-tuple-element.372), branch_computations={%region_26.27_spmd, %region_27.28_spmd} | conditional | bytes 6684776 | solution.py:56
  273.0 4.3 collective-permute-start.22
  281.9 34.5 %conditional.36 = ((bf16[1024,512]{1,0:T(8,128)(2,1)}, bf16[1024,32]{1,0:T(8,128)(2,1)})) conditional(s32[]{:T(128)} %bitcast.13, (bf16[1024,512]{1,0:T(8,128)(2,1)}, bf16[1024,32]{1,0:T(8,128)(2,1)}) %get-tuple-element.373, (bf16[1024,512]{1,0:T(8,128)(2,1)}, bf16[1024,32]{1,0:T(8,128)(2,1)}) %get-tuple-element.373), branch_computations={%region_28.29_spmd, %region_29.30_spmd} | conditional | bytes 6684776 | solution.py:56
  281.9 3.7 collective-permute-start.24
  285.6 29.0 %collective-permute-done.25 = bf16[1024,32]{1,0:T(8,128)(2,1)S(1)} collective-permute-done((bf16[1024,32]{1,0:T(8,128)(2,1)}, bf16[1024,32]{1,0:T(8,128)(2,1)S(1)}, u32[]{:S(2)}, u32[]{:S(2)}) %collective-permute-start.25) | collective-permute-done | bytes 65568 | tf_op jit(solution)/shard_map/cond/branch_1_fun/ppermute | solution.py:29
  316.3 32.8 %conditional.39 = ((bf16[1024,512]{1,0:T(8,128)(2,1)}, bf16[1024,32]{1,0:T(8,128)(2,1)})) conditional(s32[]{:T(128)} %bitcast.10, (bf16[1024,512]{1,0:T(8,128)(2,1)}, bf16[1024,32]{1,0:T(8,128)(2,1)}) %get-tuple-element.376, (bf16[1024,512]{1,0:T(8,128)(2,1)}, bf16[1024,32]{1,0:T(8,128)(2,1)}) %get-tuple-element.376), branch_computations={%region_34.35_spmd, %region_35.36_spmd} | conditional | bytes 6684776 | solution.py:56
  319.3 28.2 %collective-permute-done.31 = bf16[1024,32]{1,0:T(8,128)(2,1)S(1)} collective-permute-done((bf16[1024,32]{1,0:T(8,128)(2,1)}, bf16[1024,32]{1,0:T(8,128)(2,1)S(1)}, u32[]{:S(2)}, u32[]{:S(2)}) %collective-permute-start.31) | collective-permute-done | bytes 65568 | tf_op jit(solution)/shard_map/cond/branch_1_fun/ppermute | solution.py:29
  352.4 30.5 %conditional.25 = ((bf16[1024,512]{1,0:T(8,128)(2,1)}, bf16[1024,32]{1,0:T(8,128)(2,1)})) conditional(s32[]{:T(128)} %bitcast.7, (bf16[1024,512]{1,0:T(8,128)(2,1)}, bf16[1024,32]{1,0:T(8,128)(2,1)}) %conditional.24, (bf16[1024,512]{1,0:T(8,128)(2,1)}, bf16[1024,32]{1,0:T(8,128)(2,1)}) %conditional.24), branch_computations={%region_5.6_spmd, %region_6.7_spmd} | conditional | bytes 6684776 | solution.py:56
  353.9 27.2 %collective-permute-done.3 = bf16[1024,32]{1,0:T(8,128)(2,1)S(1)} collective-permute-done((bf16[1024,32]{1,0:T(8,128)(2,1)}, bf16[1024,32]{1,0:T(8,128)(2,1)S(1)}, u32[]{:S(2)}, u32[]{:S(2)}) %collective-permute-start.3) | collective-permute-done | bytes 65568 | tf_op jit(solution)/shard_map/cond/branch_1_fun/ppermute | solution.py:29
  382.9 7.3 %conditional.27 = ((bf16[1024,512]{1,0:T(8,128)(2,1)}, bf16[1024,32]{1,0:T(8,128)(2,1)})) conditional(s32[]{:T(128)} %bitcast.5, (bf16[1024,512]{1,0:T(8,128)(2,1)}, bf16[1024,32]{1,0:T(8,128)(2,1)}) %get-tuple-element.365, (bf16[1024,512]{1,0:T(8,128)(2,1)}, bf16[1024,32]{1,0:T(8,128)(2,1)}) %get-tuple-element.365), branch_computations={%region_9.10_spmd, %region_10.11_spmd} | conditional | bytes 6684776 | solution.py:56
  390.2 33.5 %conditional.31 = ((bf16[1024,512]{1,0:T(8,128)(2,1)}, bf16[1024,32]{1,0:T(8,128)(2,1)})) conditional(s32[]{:T(128)} %bitcast.1, (bf16[1024,512]{1,0:T(8,128)(2,1)}, bf16[1024,32]{1,0:T(8,128)(2,1)}) %get-tuple-element.369, (bf16[1024,512]{1,0:T(8,128)(2,1)}, bf16[1024,32]{1,0:T(8,128)(2,1)}) %get-tuple-element.369), branch_computations={%region_17.18_spmd, %region_18.19_spmd} | conditional | bytes 6684776 | solution.py:56
  393.2 28.7 %collective-permute-done.15 = bf16[1024,32]{1,0:T(8,128)(2,1)S(1)} collective-permute-done((bf16[1024,32]{1,0:T(8,128)(2,1)}, bf16[1024,32]{1,0:T(8,128)(2,1)S(1)}, u32[]{:S(2)}, u32[]{:S(2)}) %collective-permute-start.15) | collective-permute-done | bytes 65568 | tf_op jit(solution)/shard_map/cond/branch_1_fun/ppermute | solution.py:29
  432.1 4.5 multiply_bitcast_fusion
  436.6 5.5 copy.13
  442.1 3.5 multiply_reduce_fusion.5
  445.6 78.1 %all-reduce = (f32[32]{0:T(128)S(1)}, f32[32]{0:T(128)S(1)}) all-reduce(f32[32]{0:T(128)S(1)} %multiply_reduce_fusion.6, f32[32]{0:T(128)S(1)} %get-tuple-element.264), channel_id=1, replica_groups=mesh['blk'=32,'grp'=8] {'blk','grp'}, use_global_device_ids=true, to_apply=%region_1.2 | all-reduce | flops 64 | bytes 512 | tf_op jit(solution)/shard_map/psum | solution.py:77
  523.9 72.4 %psum.23 = f32[32]{0:T(128)S(1)} all-reduce(f32[32]{0:T(128)S(1)} %get-tuple-element.257), channel_id=1, replica_groups=mesh['blk'=32,'grp'=8] {'blk','grp'}, use_global_device_ids=true, to_apply=%region_57.58 | all-reduce | flops 32 | bytes 256 | tf_op jit(solution)/shard_map/psum | solution.py:81
  (103 shorter events, 76.9 us)
Async XLA Ops:
  20.3 29.5 %collective-permute-start.32 = (bf16[1024,512]{1,0:T(8,128)(2,1)}, bf16[1024,512]{1,0:T(8,128)(2,1)}, u32[]{:S(2)}, u32[]{:S(2)}) collective-permute-start(bf16[1024,512]{1,0:T(8,128)(2,1)} %get-tuple-element.224), channel_id=1, source_target_pairs={{0,1},{1,0},{2,3},{3,2},{4,5},{5,4},{6,7},{7,6},{8,9},{9,8},{10,11... | collective-permute-start | bytes 3145736 | tf_op jit(solution)/shard_map/cond/branch_1_fun/ppermute | solution.py:29
  22.5 27.4 %collective-permute-start.33 = (bf16[1024,32]{1,0:T(8,128)(2,1)S(1)}, bf16[1024,32]{1,0:T(8,128)(2,1)}, u32[]{:S(2)}, u32[]{:S(2)}) collective-permute-start(bf16[1024,32]{1,0:T(8,128)(2,1)S(1)} %get-tuple-element.225), channel_id=1, source_target_pairs={{0,1},{1,0},{2,3},{3,2},{4,5},{5,4},{6,7},{7,6},{8,9},{9,8},{10,11... | collective-permute-start | bytes 196616 | tf_op jit(solution)/shard_map/cond/branch_1_fun/ppermute | solution.py:29
  49.8 30.9 %collective-permute-start.34 = (bf16[1024,512]{1,0:T(8,128)(2,1)}, bf16[1024,512]{1,0:T(8,128)(2,1)S(1)}, u32[]{:S(2)}, u32[]{:S(2)}) collective-permute-start(bf16[1024,512]{1,0:T(8,128)(2,1)} %get-tuple-element.226), channel_id=1, source_target_pairs={{0,2},{2,0},{1,3},{3,1},{4,6},{6,4},{5,7},{7,5},{8,10},{10,8},{9,1... | collective-permute-start | bytes 3145736 | tf_op jit(solution)/shard_map/cond/branch_1_fun/ppermute | solution.py:29
  52.5 27.5 %collective-permute-start.35 = (bf16[1024,32]{1,0:T(8,128)(2,1)}, bf16[1024,32]{1,0:T(8,128)(2,1)S(1)}, u32[]{:S(2)}, u32[]{:S(2)}) collective-permute-start(bf16[1024,32]{1,0:T(8,128)(2,1)} %get-tuple-element.227), channel_id=1, source_target_pairs={{0,2},{2,0},{1,3},{3,1},{4,6},{6,4},{5,7},{7,5},{8,10},{10,8},{9,1... | collective-permute-start | bytes 196616 | tf_op jit(solution)/shard_map/cond/branch_1_fun/ppermute | solution.py:29
  81.8 6.0 %collective-permute-start.38 = (bf16[1024,512]{1,0:T(8,128)(2,1)}, bf16[1024,512]{1,0:T(8,128)(2,1)S(1)}, u32[]{:S(2)}, u32[]{:S(2)}) collective-permute-start(bf16[1024,512]{1,0:T(8,128)(2,1)} %get-tuple-element.230), channel_id=1, source_target_pairs={{0,8},{8,0},{1,9},{9,1},{2,10},{10,2},{3,11},{11,3},{4,12},{12,4},... | collective-permute-start | bytes 3145736 | tf_op jit(solution)/shard_map/cond/branch_1_fun/ppermute | solution.py:29
  84.2 2.9 collective-permute-start.39
  88.8 31.6 %collective-permute-start.40 = (bf16[1024,512]{1,0:T(8,128)(2,1)}, bf16[1024,512]{1,0:T(8,128)(2,1)S(1)}, u32[]{:S(2)}, u32[]{:S(2)}) collective-permute-start(bf16[1024,512]{1,0:T(8,128)(2,1)} %get-tuple-element.232), channel_id=1, source_target_pairs={{0,16},{16,0},{1,17},{17,1},{2,18},{18,2},{3,19},{19,3},{4,20},{20... | collective-permute-start | bytes 3145736 | tf_op jit(solution)/shard_map/cond/branch_1_fun/ppermute | solution.py:29
  90.6 29.1 %collective-permute-start.41 = (bf16[1024,32]{1,0:T(8,128)(2,1)}, bf16[1024,32]{1,0:T(8,128)(2,1)S(1)}, u32[]{:S(2)}, u32[]{:S(2)}) collective-permute-start(bf16[1024,32]{1,0:T(8,128)(2,1)} %get-tuple-element.233), channel_id=1, source_target_pairs={{0,16},{16,0},{1,17},{17,1},{2,18},{18,2},{3,19},{19,3},{4,20},{20... | collective-permute-start | bytes 196616 | tf_op jit(solution)/shard_map/cond/branch_1_fun/ppermute | solution.py:29
  121.3 93.3 %copy-start = (bf16[1024,512]{1,0:T(8,128)(2,1)S(1)}, bf16[1024,512]{1,0:T(8,128)(2,1)}, u32[]{:S(2)}) copy-start(bf16[1024,512]{1,0:T(8,128)(2,1)} %param.55) | copy-start | bytes 3145732
  121.3 60.1 %collective-permute-start.42 = (bf16[1024,512]{1,0:T(8,128)(2,1)}, bf16[1024,512]{1,0:T(8,128)(2,1)S(1)}, u32[]{:S(2)}, u32[]{:S(2)}) collective-permute-start(bf16[1024,512]{1,0:T(8,128)(2,1)} %get-tuple-element.234), channel_id=1, source_target_pairs={{0,32},{32,0},{1,33},{33,1},{2,34},{34,2},{3,35},{35,3},{4,36},{36... | collective-permute-start | bytes 3145736 | tf_op jit(solution)/shard_map/cond/branch_1_fun/ppermute | solution.py:29
  124.2 56.5 %collective-permute-start.43 = (bf16[1024,32]{1,0:T(8,128)(2,1)}, bf16[1024,32]{1,0:T(8,128)(2,1)S(1)}, u32[]{:S(2)}, u32[]{:S(2)}) collective-permute-start(bf16[1024,32]{1,0:T(8,128)(2,1)} %get-tuple-element.235), channel_id=1, source_target_pairs={{0,32},{32,0},{1,33},{33,1},{2,34},{34,2},{3,35},{35,3},{4,36},{36... | collective-permute-start | bytes 196616 | tf_op jit(solution)/shard_map/cond/branch_1_fun/ppermute | solution.py:29
  182.4 31.2 %collective-permute-start.46 = (bf16[1024,512]{1,0:T(8,128)(2,1)}, bf16[1024,512]{1,0:T(8,128)(2,1)S(1)}, u32[]{:S(2)}, u32[]{:S(2)}) collective-permute-start(bf16[1024,512]{1,0:T(8,128)(2,1)} %get-tuple-element.238), channel_id=1, source_target_pairs={{0,128},{128,0},{1,129},{129,1},{2,130},{130,2},{3,131},{131,3},{4... | collective-permute-start | bytes 3145736 | tf_op jit(solution)/shard_map/cond/branch_1_fun/ppermute | solution.py:29
  185.2 27.7 %collective-permute-start.47 = (bf16[1024,32]{1,0:T(8,128)(2,1)}, bf16[1024,32]{1,0:T(8,128)(2,1)S(1)}, u32[]{:S(2)}, u32[]{:S(2)}) collective-permute-start(bf16[1024,32]{1,0:T(8,128)(2,1)} %get-tuple-element.239), channel_id=1, source_target_pairs={{0,128},{128,0},{1,129},{129,1},{2,130},{130,2},{3,131},{131,3},{4... | collective-permute-start | bytes 196616 | tf_op jit(solution)/shard_map/cond/branch_1_fun/ppermute | solution.py:29
  216.2 28.0 %collective-permute-start.16 = (bf16[1024,512]{1,0:T(8,128)(2,1)S(1)}, bf16[1024,512]{1,0:T(8,128)(2,1)}, u32[]{:S(2)}, u32[]{:S(2)}) collective-permute-start(bf16[1024,512]{1,0:T(8,128)(2,1)S(1)} %get-tuple-element.208), channel_id=1, source_target_pairs={{0,1},{1,0},{2,3},{3,2},{4,5},{5,4},{6,7},{7,6},{8,9},{9,8},{10,11... | collective-permute-start | bytes 3145736 | tf_op jit(solution)/shard_map/cond/branch_1_fun/ppermute | solution.py:29
  217.5 26.7 %collective-permute-start.17 = (bf16[1024,32]{1,0:T(8,128)(2,1)S(1)}, bf16[1024,32]{1,0:T(8,128)(2,1)}, u32[]{:S(2)}, u32[]{:S(2)}) collective-permute-start(bf16[1024,32]{1,0:T(8,128)(2,1)S(1)} %get-tuple-element.209), channel_id=1, source_target_pairs={{0,1},{1,0},{2,3},{3,2},{4,5},{5,4},{6,7},{7,6},{8,9},{9,8},{10,11... | collective-permute-start | bytes 196616 | tf_op jit(solution)/shard_map/cond/branch_1_fun/ppermute | solution.py:29
  244.2 27.8 %collective-permute-start.18 = (bf16[1024,512]{1,0:T(8,128)(2,1)}, bf16[1024,512]{1,0:T(8,128)(2,1)S(1)}, u32[]{:S(2)}, u32[]{:S(2)}) collective-permute-start(bf16[1024,512]{1,0:T(8,128)(2,1)} %get-tuple-element.210), channel_id=1, source_target_pairs={{0,2},{2,0},{1,3},{3,1},{4,6},{6,4},{5,7},{7,5},{8,10},{10,8},{9,1... | collective-permute-start | bytes 3145736 | tf_op jit(solution)/shard_map/cond/branch_1_fun/ppermute | solution.py:29
  245.5 25.8 %collective-permute-start.19 = (bf16[1024,32]{1,0:T(8,128)(2,1)}, bf16[1024,32]{1,0:T(8,128)(2,1)S(1)}, u32[]{:S(2)}, u32[]{:S(2)}) collective-permute-start(bf16[1024,32]{1,0:T(8,128)(2,1)} %get-tuple-element.211), channel_id=1, source_target_pairs={{0,2},{2,0},{1,3},{3,1},{4,6},{6,4},{5,7},{7,5},{8,10},{10,8},{9,1... | collective-permute-start | bytes 196616 | tf_op jit(solution)/shard_map/cond/branch_1_fun/ppermute | solution.py:29
  273.0 7.8 %collective-permute-start.22 = (bf16[1024,512]{1,0:T(8,128)(2,1)}, bf16[1024,512]{1,0:T(8,128)(2,1)S(1)}, u32[]{:S(2)}, u32[]{:S(2)}) collective-permute-start(bf16[1024,512]{1,0:T(8,128)(2,1)} %get-tuple-element.214), channel_id=1, source_target_pairs={{0,8},{8,0},{1,9},{9,1},{2,10},{10,2},{3,11},{11,3},{4,12},{12,4},... | collective-permute-start | bytes 3145736 | tf_op jit(solution)/shard_map/cond/branch_1_fun/ppermute | solution.py:29
  277.3 2.9 collective-permute-start.23
  281.9 33.5 %collective-permute-start.24 = (bf16[1024,512]{1,0:T(8,128)(2,1)}, bf16[1024,512]{1,0:T(8,128)(2,1)S(1)}, u32[]{:S(2)}, u32[]{:S(2)}) collective-permute-start(bf16[1024,512]{1,0:T(8,128)(2,1)} %get-tuple-element.216), channel_id=1, source_target_pairs={{0,16},{16,0},{1,17},{17,1},{2,18},{18,2},{3,19},{19,3},{4,20},{20... | collective-permute-start | bytes 3145736 | tf_op jit(solution)/shard_map/cond/branch_1_fun/ppermute | solution.py:29
  285.6 29.1 %collective-permute-start.25 = (bf16[1024,32]{1,0:T(8,128)(2,1)}, bf16[1024,32]{1,0:T(8,128)(2,1)S(1)}, u32[]{:S(2)}, u32[]{:S(2)}) collective-permute-start(bf16[1024,32]{1,0:T(8,128)(2,1)} %get-tuple-element.217), channel_id=1, source_target_pairs={{0,16},{16,0},{1,17},{17,1},{2,18},{18,2},{3,19},{19,3},{4,20},{20... | collective-permute-start | bytes 196616 | tf_op jit(solution)/shard_map/cond/branch_1_fun/ppermute | solution.py:29
  316.3 31.8 %collective-permute-start.30 = (bf16[1024,512]{1,0:T(8,128)(2,1)}, bf16[1024,512]{1,0:T(8,128)(2,1)S(1)}, u32[]{:S(2)}, u32[]{:S(2)}) collective-permute-start(bf16[1024,512]{1,0:T(8,128)(2,1)} %get-tuple-element.222), channel_id=1, source_target_pairs={{0,128},{128,0},{1,129},{129,1},{2,130},{130,2},{3,131},{131,3},{4... | collective-permute-start | bytes 3145736 | tf_op jit(solution)/shard_map/cond/branch_1_fun/ppermute | solution.py:29
  319.1 28.4 %collective-permute-start.31 = (bf16[1024,32]{1,0:T(8,128)(2,1)}, bf16[1024,32]{1,0:T(8,128)(2,1)S(1)}, u32[]{:S(2)}, u32[]{:S(2)}) collective-permute-start(bf16[1024,32]{1,0:T(8,128)(2,1)} %get-tuple-element.223), channel_id=1, source_target_pairs={{0,128},{128,0},{1,129},{129,1},{2,130},{130,2},{3,131},{131,3},{4... | collective-permute-start | bytes 196616 | tf_op jit(solution)/shard_map/cond/branch_1_fun/ppermute | solution.py:29
  352.4 29.4 %collective-permute-start.2 = (bf16[1024,512]{1,0:T(8,128)(2,1)}, bf16[1024,512]{1,0:T(8,128)(2,1)S(1)}, u32[]{:S(2)}, u32[]{:S(2)}) collective-permute-start(bf16[1024,512]{1,0:T(8,128)(2,1)} %get-tuple-element.194), channel_id=1, source_target_pairs={{0,2},{2,0},{1,3},{3,1},{4,6},{6,4},{5,7},{7,5},{8,10},{10,8},{9,1... | collective-permute-start | bytes 3145736 | tf_op jit(solution)/shard_map/cond/branch_1_fun/ppermute | solution.py:29
  353.7 27.4 %collective-permute-start.3 = (bf16[1024,32]{1,0:T(8,128)(2,1)}, bf16[1024,32]{1,0:T(8,128)(2,1)S(1)}, u32[]{:S(2)}, u32[]{:S(2)}) collective-permute-start(bf16[1024,32]{1,0:T(8,128)(2,1)} %get-tuple-element.195), channel_id=1, source_target_pairs={{0,2},{2,0},{1,3},{3,1},{4,6},{6,4},{5,7},{7,5},{8,10},{10,8},{9,1... | collective-permute-start | bytes 196616 | tf_op jit(solution)/shard_map/cond/branch_1_fun/ppermute | solution.py:29
  382.9 6.3 %collective-permute-start.6 = (bf16[1024,512]{1,0:T(8,128)(2,1)}, bf16[1024,512]{1,0:T(8,128)(2,1)S(1)}, u32[]{:S(2)}, u32[]{:S(2)}) collective-permute-start(bf16[1024,512]{1,0:T(8,128)(2,1)} %get-tuple-element.198), channel_id=1, source_target_pairs={{0,8},{8,0},{1,9},{9,1},{2,10},{10,2},{3,11},{11,3},{4,12},{12,4},... | collective-permute-start | bytes 3145736 | tf_op jit(solution)/shard_map/cond/branch_1_fun/ppermute | solution.py:29
  385.6 2.9 collective-permute-start.7
  390.2 32.4 %collective-permute-start.14 = (bf16[1024,512]{1,0:T(8,128)(2,1)}, bf16[1024,512]{1,0:T(8,128)(2,1)S(1)}, u32[]{:S(2)}, u32[]{:S(2)}) collective-permute-start(bf16[1024,512]{1,0:T(8,128)(2,1)} %get-tuple-element.206), channel_id=1, source_target_pairs={{0,128},{128,0},{1,129},{129,1},{2,130},{130,2},{3,131},{131,3},{4... | collective-permute-start | bytes 3145736 | tf_op jit(solution)/shard_map/cond/branch_1_fun/ppermute | solution.py:29
  393.0 28.9 %collective-permute-start.15 = (bf16[1024,32]{1,0:T(8,128)(2,1)}, bf16[1024,32]{1,0:T(8,128)(2,1)S(1)}, u32[]{:S(2)}, u32[]{:S(2)}) collective-permute-start(bf16[1024,32]{1,0:T(8,128)(2,1)} %get-tuple-element.207), channel_id=1, source_target_pairs={{0,128},{128,0},{1,129},{129,1},{2,130},{130,2},{3,131},{131,3},{4... | collective-permute-start | bytes 196616 | tf_op jit(solution)/shard_map/cond/branch_1_fun/ppermute | solution.py:29
  442.1 81.6 %copy-start.3 = (f32[1024,32]{0,1:T(8,128)S(1)}, f32[1024,32]{0,1:T(8,128)}, u32[]{:S(2)}) copy-start(f32[1024,32]{0,1:T(8,128)} %param.57) | copy-start | bytes 393220
  442.1 154.3 %copy-start.4 = (f32[1024,32]{0,1:T(8,128)S(1)}, f32[1024,32]{0,1:T(8,128)}, u32[]{:S(2)}) copy-start(f32[1024,32]{0,1:T(8,128)} %param.58) | copy-start | bytes 393220
  523.9 73.2 %copy-start.2 = (f32[1024,32]{0,1:T(8,128)}, f32[1024,32]{0,1:T(8,128)S(1)}, u32[]{:S(2)}) copy-start(f32[1024,32]{0,1:T(8,128)S(1)} %get-tuple-element.258) | copy-start | bytes 393220
  (2 other events, 11.0 us)
where the time goes:
time: 598 us; the launch traced here: 597 us
  waiting for transfers between devices  342 us (57%)
  blocking collectives  151 us (25%)
  starting transfers between devices  36.2 us (6%)
  local copies, waits for them, and re-layouts  30.3 us (5%)
  between operations  16.9 us (3%)
  matrix products  14.6 us (2%)
  other arithmetic  6.71 us (1%)
    ppermute x28, waiting for transfers between devices, from_partner(): return lax.ppermute(block, axis, route)  342 us
    psum x1, blocking collectives, local(): norm_now, curvature = lax.psum((local_norm, local_curv), ('blk', 'grp'))  78.1 us
    psum x1, blocking collectives, local(): lax.psum(jnp.sum(new_residual * new_residual, axis=0), ('blk', 'grp'))  72.4 us
    ppermute x28, starting transfers between devices, from_partner(): return lax.ppermute(block, axis, route)  36.2 us
    cond x26, local copies, waits for them, and re-layouts  22.3 us
  transfers between devices with their start and end apart: 28, of which 14 were waited for; matrix products, arithmetic and copies ran while one was open for 1% of the time, Pallas kernels for 0%

commit v1 on v0

v1 whole, which is shorter than its diff:
```python
import functools
import math

import jax
import jax.numpy as jnp
from jax import lax
from jax.experimental import pallas as pl
from jax.experimental.pallas import tpu as pltpu
from jax.sharding import PartitionSpec as P

ROUNDS = 3
GAMMA = 2.0
ROWS = 1024
DIM = 512
PROBES = 32
AXES = ("blk", "grp")
MESH = pl.DeviceIdType.MESH
VMEM = pl.BlockSpec(memory_space=pltpu.VMEM)
F32 = jnp.float32
BF16 = jnp.bfloat16
TALL = ROWS + 2 * PROBES
TILE = 256
CORE = 8
SCALE = -GAMMA * math.log2(math.e)
LOSS = 1e-2


def params(collective_id=None):
    return pltpu.CompilerParams(
        collective_id=collective_id,
        has_side_effects=collective_id is not None,
        vmem_limit_bytes=40 * 2**20,
    )


def prepare_kernel(x_ref, d_ref, both_ref, xt_ref, sq_ref, send_sem, recv_sem):
    blk, grp = lax.axis_index("blk"), lax.axis_index("grp")
    other = (blk ^ 1, grp)
    barrier = pltpu.get_barrier_semaphore()
    pl.semaphore_signal(barrier, inc=1, device_id=other, device_id_type=MESH)
    both_ref[0, :ROWS] = x_ref[...]
    low = d_ref[...].astype(BF16)
    both_ref[0, ROWS : ROWS + PROBES] = low[:, :DIM]
    both_ref[0, ROWS + PROBES :] = low[:, DIM:]
    pl.semaphore_wait(barrier, 1)
    copy = pltpu.make_async_remote_copy(
        src_ref=both_ref.at[0],
        dst_ref=both_ref.at[1],
        send_sem=send_sem,
        recv_sem=recv_sem,
        device_id=other,
        device_id_type=MESH,
    )
    copy.start()
    xt = x_ref[...].T
    xt_ref[...] = xt
    wide = xt.astype(F32)
    sq_ref[...] = jnp.sum(wide * wide, axis=0, keepdims=True)
    copy.wait()


def prepare(embedding, dir_t):
    return pl.pallas_call(
        prepare_kernel,
        out_shape=(
            jax.ShapeDtypeStruct((2, TALL, DIM), BF16),
            jax.ShapeDtypeStruct((DIM, ROWS), BF16),
            jax.ShapeDtypeStruct((1, ROWS), F32),
        ),
        in_specs=[VMEM] * 2,
        out_specs=(VMEM,) * 3,
        scratch_shapes=[pltpu.SemaphoreType.DMA, pltpu.SemaphoreType.DMA],
        compiler_params=params(1),
        name="prepare",
    )(embedding, dir_t)


def product_kernel(xt_ref, sq_ref, y_ref, acc_ref, out_ref):
    total = acc_ref[...]
    for tile in range(ROWS // TILE):
        part = y_ref[tile * TILE : (tile + 1) * TILE, :]
        wide = part.astype(F32)
        part_sq = jnp.sum(wide * wide, axis=1, keepdims=True)
        cross = jnp.dot(part, xt_ref[...], preferred_element_type=F32)
        dist = part_sq + sq_ref[...] - 2.0 * cross
        kern = jnp.exp2(SCALE * dist + 1.0).astype(BF16)
        half, column = divmod(tile * TILE, DIM)
        row = ROWS + half * PROBES
        probe = y_ref[row : row + PROBES, column : column + TILE]
        total = total + jnp.dot(probe, kern, preferred_element_type=F32)
    out_ref[...] = total


def product(xt, sq, partner, acc):
    return pl.pallas_call(
        product_kernel,
        out_shape=jax.ShapeDtypeStruct((PROBES, ROWS), F32),
        in_specs=[VMEM] * 4,
        out_specs=VMEM,
        compiler_params=params(),
        name="product",
    )(xt, sq, partner, acc)


def tree(ref):
    v = ref[...]
    while v.shape[0] > 1:
        half = v.shape[0] // 2
        v = v[:half] + v[half:]
    return v[0]


def exchange(slots, send_sem, recv_sem, place):
    count = slots.shape[0]
    for k in range(1, count):
        pltpu.make_async_remote_copy(
            src_ref=slots.at[0],
            dst_ref=slots.at[k],
            send_sem=send_sem,
            recv_sem=recv_sem,
            device_id=place(k),
            device_id_type=MESH,
        ).start()
    whole = pltpu.make_async_remote_copy(
        src_ref=slots.at[pl.ds(1, count - 1)],
        dst_ref=slots.at[pl.ds(1, count - 1)],
        send_sem=send_sem,
        recv_sem=recv_sem,
        device_id=place(1),
        device_id_type=MESH,
    )
    whole.wait_recv()
    return whole


def finish_kernel(
    d_ref, r_ref, s_ref, p_ref, acc_ref, ns_ref, nr_ref, nd_ref, bad_ref,
    near, far, near_send, near_recv, far_send, far_recv,
):
    blk, grp = lax.axis_index("blk"), lax.axis_index("grp")

    def near_place(k):
        return (blk ^ (k >> 3), grp ^ (k & 7))

    def far_place(k):
        return (blk ^ (k << 1), grp)

    barrier = pltpu.get_barrier_semaphore()
    for k in range(1, 16):
        pl.semaphore_signal(barrier, inc=1, device_id=near_place(k), device_id_type=MESH)
        pl.semaphore_signal(barrier, inc=1, device_id=far_place(k), device_id_type=MESH)
    d, r = d_ref[...], r_ref[...]
    image = p_ref[...] + acc_ref[...] + d
    columns = [
        jnp.sum(a * b, axis=1, keepdims=True)
        for a, b in ((r, r), (d, image), (r, image), (image, image))
    ]
    lane = lax.broadcasted_iota(jnp.int32, (8, 128), 1)
    packed = jnp.zeros((8, 128), F32)
    for q, column in enumerate(columns):
        for g in range(4):
            packed = jnp.where(lane == q * 4 + g, column[g * 8 : g * 8 + 8], packed)
    near[0] = packed
    pl.semaphore_wait(barrier, 30)
    first = exchange(near, near_send, near_recv, near_place)
    far[0] = tree(near)
    second = exchange(far, far_send, far_recv, far_place)
    total = tree(far)
    norm, curv, cross, square = (
        jnp.concatenate([total[:, q * 4 + g : q * 4 + g + 1] for g in range(4)], axis=0)
        for q in range(4)
    )
    alpha = norm / curv
    ns_ref[...] = s_ref[...] + alpha * d
    new_residual = r - alpha * image
    nr_ref[...] = new_residual
    twice, quad = 2.0 * alpha * cross, alpha * alpha * square
    following = norm - twice + quad
    good = following >= LOSS * (norm + jnp.abs(twice) + quad)
    good = jnp.logical_and(good, following < 3e38)
    nd_ref[...] = new_residual + (following / norm) * d
    bad = jnp.where(good, 0.0, 1.0)
    bad_ref[0, 0] = jnp.max(bad)
    bad_ref[0, 1] = 0.0
    first.wait_send()
    second.wait_send()


def finish(dir_t, res_t, sol_t, prior_t, acc):
    shape = jax.ShapeDtypeStruct((PROBES, ROWS), F32)
    return pl.pallas_call(
        finish_kernel,
        out_shape=(shape, shape, shape, jax.ShapeDtypeStruct((1, 2), F32)),
        in_specs=[VMEM] * 5,
        out_specs=(VMEM, VMEM, VMEM, pl.BlockSpec(memory_space=pltpu.SMEM)),
        scratch_shapes=[pltpu.VMEM((16, 8, 128), F32)] * 2 + [pltpu.SemaphoreType.DMA] * 4,
        compiler_params=params(2),
        name="finish",
    )(dir_t, res_t, sol_t, prior_t, acc)


def move_branches(count):
    def branch(chips):
        if chips == 0:
            return lambda block: block
        mask = (chips >> 3) << 4 | (chips & 7)
        route = [(i, i ^ mask) for i in range(count)]
        return lambda block: lax.ppermute(block, AXES, route)

    return [branch(chips) for chips in range(count // 2)]


def local(embedding, direction, residual, solution, prior, plan, round_index):
    count = lax.axis_size(AXES)
    branches = move_branches(count)
    dir_t, res_t = direction.T, residual.T
    both, xt, sq = prepare(embedding, dir_t)
    masks = lax.dynamic_slice(plan, (round_index[0],), (ROUNDS,))

    def one_round(step, acc):
        mask = masks[step]
        core = jnp.bitwise_and(mask >> 3, 1)
        chips = jnp.bitwise_or((mask >> 4) << 3, jnp.bitwise_and(mask, 7))
        block = lax.dynamic_index_in_dim(both, core, 0, keepdims=False)
        partner = lax.switch(chips, branches, block)
        return product(xt, sq, partner, acc)

    acc = lax.fori_loop(0, ROUNDS, one_round, jnp.zeros((PROBES, ROWS), F32))
    new_sol, new_res, new_dir, bad = finish(dir_t, res_t, solution.T, prior.T, acc)

    def again(new_dir):
        norm = lax.psum(jnp.sum(res_t * res_t, axis=1, keepdims=True), AXES)
        following = lax.psum(jnp.sum(new_res * new_res, axis=1, keepdims=True), AXES)
        return new_res + following / norm * dir_t

    new_dir = lax.cond(bad[0, 0] > 0, again, lambda v: v, new_dir)
    return new_sol.T, new_res.T, new_dir.T


def solution(mesh):
    rows = P(AXES, None)
    return jax.shard_map(
        local,
        mesh=mesh,
        in_specs=(rows,) * 5 + (P(), P()),
        out_specs=(rows,) * 3,
        check_vma=False,
    )
```

time: 598 us -> 281 us (0.47)
  waiting for transfers between devices: 342 us -> 89.8 us
  blocking collectives: 151 us -> 0 us
  loops' own time: 0.11 us -> 102 us
  Pallas kernels: 0 us -> 67.3 us
  starting transfers between devices: 36.2 us -> 8.85 us
  local copies, waits for them, and re-layouts: 30.3 us -> 9.97 us
  between operations: 16.9 us -> 1.65 us
  matrix products: 14.6 us -> 0 us
  other arithmetic: 6.71 us -> 0 us
    ppermute x28 -> x3, waiting for transfers between devices: 342 us -> 89.8 us  [branch(): return lambda block: lax.ppermute(block, AXES, route)]
    psum x2 -> x0, blocking collectives: 151 us -> none  [the longest x1 78.1 us: local(): norm_now, curvature = lax.psum((local_norm, local_curv), ('blk', 'grp'))]
    another operation x24 -> x5, loops' own time: 0.11 us -> 102 us  [the longest x3 74.6 us: one_round(): partner = lax.switch(chips, branches, block)]
    pallas_call x0 -> x5, Pallas kernels: none -> 67.3 us  [the longest x1 40.5 us: finish(): pl.pallas_call(finish_kernel, out_shape=(shape, shape, shape, jax.ShapeDt...]
    ppermute x28 -> x3, starting transfers between devices: 36.2 us -> 8.85 us  [branch(): return lambda block: lax.ppermute(block, AXES, route)]
    cond x26 -> x3, local copies, waits for them, and re-layouts: 22.3 us -> 0.22 us
    dot_general x4 -> x0, matrix products: 14.6 us -> none  [the longest x3 10.1 us: local(): jnp.dot(kern, partner_dir, preferred_element_type=jnp.float32)]
  transfers between devices with their start and end apart: 28 -> 3, of which waited for: 14 -> 3; matrix products, arithmetic and copies ran while one was open for 1% -> 0% of each run, Pallas kernels for 0% -> 0%
where the time goes in v1:
time: 281 us; the launch traced here: 280 us
  loops' own time  102 us (36%)
  waiting for transfers between devices  89.8 us (32%)
  Pallas kernels  67.3 us (24%)
  local copies, waits for them, and re-layouts  9.97 us (4%)
  starting transfers between devices  8.85 us (3%)
    ppermute x3, waiting for transfers between devices, branch(): return lambda block: lax.ppermute(block, AXES, route)  89.8 us
    another operation x3, loops' own time, one_round(): partner = lax.switch(chips, branches, block)  74.6 us
    pallas_call x1, Pallas kernels, finish(): pl.pallas_call(finish_kernel, out_shape=(shape, shape, shape, jax.ShapeDt...  40.5 us
    another operation x1, loops' own time, local(): acc = lax.fori_loop(0, ROUNDS, one_round, jnp.zeros((PROBES, ROWS), F32))  27.5 us
    pallas_call x1, Pallas kernels, prepare(): pl.pallas_call(prepare_kernel, out_shape=(jax.ShapeDtypeStruct((2, TALL,...  20.5 us
    ppermute x3, starting transfers between devices, branch(): return lambda block: lax.ppermute(block, AXES, route)  8.85 us
    pallas_call x3, Pallas kernels, product(): pl.pallas_call(product_kernel, out_shape=jax.ShapeDtypeStruct((PROBES, RO...  6.31 us
  transfers between devices with their start and end apart: 3, of which 3 were waited for; matrix products, arithmetic and copies ran while one was open for 0% of the time, Pallas kernels for 0%

profile of v1, /device:TPU:1, one launch (start us, length us, event | category | flops | bytes accessed | tf_op | source)
XLA Modules:
  0.0 279.7 jit_solution(16201219946928089788)
XLA Ops:
  1.3 0.8 dynamic_slice.18
  2.0 1.2 copy-done
  3.3 20.5 %prepare.1 = (bf16[2,1088,512]{2,1,0:T(8,128)(2,1)}, bf16[512,1024]{1,0:T(8,128)(2,1)S(1)}, f32[1,1024]{1,0:T(1,128)S(1)}) custom-call(bf16[1024,512]{1,0:T(8,128)(2,1)S(1)} %copy-done, f32[32,1024]{1,0:T(8,128)} %bitcast.31), custom_call_target="tpu_custom_call" | custom-call | tf_op jit(solution)/shard_map/prepare/pallas_call | solution.py:63
  23.7 0.0 copy-start.1
  23.8 0.0 copy-start.2
  23.8 0.0 copy-start.3
  23.8 213.0 %while.13 = (s32[]{:T(128)}, f32[32,1024]{1,0:T(8,128)S(1)}, s32[3]{0:T(128)S(1)}, bf16[2,1088,512]{2,1,0:T(8,128)(2,1)}, bf16[512,1024]{1,0:T(8,128)(2,1)S(1)},...) while((s32[]{:T(128)}, f32[32,1024]{1,0:T(8,128)S(1)}, ...), condition=%wide.region_129.130_spmd, body=%wide.region_0.129_spmd.sunk | while | flops 12 | bytes 9175375 | solution.py:228
  24.2 0.6 dynamic_slice.23
  26.7 1.3 dynamic-slice_bitcast_fusion.2
  28.0 55.1 %conditional.4 = (bf16[1088,512]{1,0:T(8,128)(2,1)S(1)}) conditional(s32[]{:T(128)} %bitcast.22, bf16[1088,512]{1,0:T(8,128)(2,1)S(1)} %dynamic-slice_bitcast_fusion.2, bf16[1088,512]{1,0:T(8,128)(2,1)S(1)} %dynamic-slice_bitcast_fusion.2, bf16[1088,512]{1,0:T(8,128)(2,1)S(1)} %dynamic-slice_bitcast_fusion.2, ...), branch_computations={%region_1.1_spmd, %region_2.2_spmd, %region_3.3_spmd, %region_4.4_... | conditional | bytes 6684720 | solution.py:225
  28.1 3.4 %collective-permute-start.12 = (bf16[1088,512]{1,0:T(8,128)(2,1)S(1)}, bf16[1088,512]{1,0:T(8,128)(2,1)S(1)}, u32[]{:S(2)}, u32[]{:S(2)}) collective-permute-start(bf16[1088,512]{1,0:T(8,128)(2,1)S(1)} %param.13), channel_id=1, source_target_pairs={{0,21},{1,20},{2,23},{3,22},{4,17},{5,16},{6,19},{7,18},{8,29},{9,... | collective-permute-start | bytes 3342344 | tf_op jit(solution)/shard_map/while/body/eval_jaxpr/cond/branch_13_fun/ppermute | solution.py:208
  31.5 25.8 %collective-permute-done.12 = bf16[1088,512]{1,0:T(8,128)(2,1)S(1)} collective-permute-done((bf16[1088,512]{1,0:T(8,128)(2,1)S(1)}, bf16[1088,512]{1,0:T(8,128)(2,1)S(1)}, u32[]{:S(2)}, u32[]{:S(2)}) %collective-permute-start.12) | collective-permute-done | bytes 1114144 | tf_op jit(solution)/shard_map/while/body/eval_jaxpr/cond/branch_13_fun/ppermute | solution.py:208
  57.3 0.1 copy.23
  83.1 2.1 product.5
  91.7 0.6 dynamic_slice.23
  94.2 1.3 dynamic-slice_bitcast_fusion.2
  95.5 51.3 %conditional.4 = (bf16[1088,512]{1,0:T(8,128)(2,1)S(1)}) conditional(s32[]{:T(128)} %bitcast.22, bf16[1088,512]{1,0:T(8,128)(2,1)S(1)} %dynamic-slice_bitcast_fusion.2, bf16[1088,512]{1,0:T(8,128)(2,1)S(1)} %dynamic-slice_bitcast_fusion.2, bf16[1088,512]{1,0:T(8,128)(2,1)S(1)} %dynamic-slice_bitcast_fusion.2, ...), branch_computations={%region_1.1_spmd, %region_2.2_spmd, %region_3.3_spmd, %region_4.4_... | conditional | bytes 6684720 | solution.py:225
  95.6 0.7 collective-permute-start.2
  96.3 25.1 %collective-permute-done.2 = bf16[1088,512]{1,0:T(8,128)(2,1)S(1)} collective-permute-done((bf16[1088,512]{1,0:T(8,128)(2,1)S(1)}, bf16[1088,512]{1,0:T(8,128)(2,1)S(1)}, u32[]{:S(2)}, u32[]{:S(2)}) %collective-permute-start.2) | collective-permute-done | bytes 1114144 | tf_op jit(solution)/shard_map/while/body/eval_jaxpr/cond/branch_3_fun/ppermute | solution.py:208
  121.4 0.1 copy.13
  146.8 2.1 product.5
  155.5 0.6 dynamic_slice.23
  158.1 1.3 dynamic-slice_bitcast_fusion.2
  159.4 67.1 %conditional.4 = (bf16[1088,512]{1,0:T(8,128)(2,1)S(1)}) conditional(s32[]{:T(128)} %bitcast.22, bf16[1088,512]{1,0:T(8,128)(2,1)S(1)} %dynamic-slice_bitcast_fusion.2, bf16[1088,512]{1,0:T(8,128)(2,1)S(1)} %dynamic-slice_bitcast_fusion.2, bf16[1088,512]{1,0:T(8,128)(2,1)S(1)} %dynamic-slice_bitcast_fusion.2, ...), branch_computations={%region_1.1_spmd, %region_2.2_spmd, %region_3.3_spmd, %region_4.4_... | conditional | bytes 6684720 | solution.py:225
  168.8 4.7 %collective-permute-start.31 = (bf16[1088,512]{1,0:T(8,128)(2,1)S(1)}, bf16[1088,512]{1,0:T(8,128)(2,1)S(1)}, u32[]{:S(2)}, u32[]{:S(2)}) collective-permute-start(bf16[1088,512]{1,0:T(8,128)(2,1)S(1)} %param.32), channel_id=1, source_target_pairs={{0,64},{1,65},{2,66},{3,67},{4,68},{5,69},{6,70},{7,71},{8,72},{9,... | collective-permute-start | bytes 3342344 | tf_op jit(solution)/shard_map/while/body/eval_jaxpr/cond/branch_32_fun/ppermute | solution.py:208
  173.5 38.9 %collective-permute-done.31 = bf16[1088,512]{1,0:T(8,128)(2,1)S(1)} collective-permute-done((bf16[1088,512]{1,0:T(8,128)(2,1)S(1)}, bf16[1088,512]{1,0:T(8,128)(2,1)S(1)}, u32[]{:S(2)}, u32[]{:S(2)}) %collective-permute-start.31) | collective-permute-done | bytes 1114144 | tf_op jit(solution)/shard_map/while/body/eval_jaxpr/cond/branch_32_fun/ppermute | solution.py:208
  212.4 0.1 copy.42
  226.4 2.1 product.5
  236.9 40.5 %finish.1 = (f32[32,1024]{1,0:T(8,128)S(1)}, f32[32,1024]{1,0:T(8,128)S(1)}, f32[32,1024]{1,0:T(8,128)S(1)}, f32[1,2]{1,0:T(1,128)S(1)}) custom-call(f32[32,1024]{1,0:T(8,128)S(1)} %bitcast.32, f32[32,1024]{1,0:T(8,128)S(1)} %bitcast.35, f32[32,1024]{1,0:T(8,128)S(1)} %bitcast.27, f32[32,1024]{1,0:T(8,128)S(1)} %bitcast.28, ...), custom_call_target="tpu_custom_call" | custom-call | tf_op jit(solution)/shard_map/finish/pallas_call | solution.py:191
  277.5 0.7 copy.152
  278.1 0.7 copy.153
  278.8 0.7 copy.154
  (11 shorter events, 0.1 us)
Async XLA Ops:
  2.0 1.2 copy-start
  23.7 213.1 %copy-start.1 = (f32[1024,32]{0,1:T(8,128)S(1)}, f32[1024,32]{0,1:T(8,128)}, u32[]{:S(2)}) copy-start(f32[1024,32]{0,1:T(8,128)} %param.142) | copy-start | bytes 393220
  23.8 213.1 %copy-start.2 = (f32[1024,32]{0,1:T(8,128)S(1)}, f32[1024,32]{0,1:T(8,128)}, u32[]{:S(2)}) copy-start(f32[1024,32]{0,1:T(8,128)} %param.143) | copy-start | bytes 393220
  23.8 213.1 %copy-start.3 = (f32[1024,32]{0,1:T(8,128)S(1)}, f32[1024,32]{0,1:T(8,128)}, u32[]{:S(2)}) copy-start(f32[1024,32]{0,1:T(8,128)} %param.140) | copy-start | bytes 393220
  23.8 213.1 %copy-start.4 = (f32[1024,32]{0,1:T(8,128)S(1)}, f32[1024,32]{0,1:T(8,128)}, u32[]{:S(2)}) copy-start(f32[1024,32]{0,1:T(8,128)} %param.141) | copy-start | bytes 393220
  28.1 29.2 %collective-permute-start.12 = (bf16[1088,512]{1,0:T(8,128)(2,1)S(1)}, bf16[1088,512]{1,0:T(8,128)(2,1)S(1)}, u32[]{:S(2)}, u32[]{:S(2)}) collective-permute-start(bf16[1088,512]{1,0:T(8,128)(2,1)S(1)} %param.13), channel_id=1, source_target_pairs={{0,21},{1,20},{2,23},{3,22},{4,17},{5,16},{6,19},{7,18},{8,29},{9,... | collective-permute-start | bytes 3342344 | tf_op jit(solution)/shard_map/while/body/eval_jaxpr/cond/branch_13_fun/ppermute | solution.py:208
  95.6 25.8 %collective-permute-start.2 = (bf16[1088,512]{1,0:T(8,128)(2,1)S(1)}, bf16[1088,512]{1,0:T(8,128)(2,1)S(1)}, u32[]{:S(2)}, u32[]{:S(2)}) collective-permute-start(bf16[1088,512]{1,0:T(8,128)(2,1)S(1)} %param.3), channel_id=1, source_target_pairs={{0,3},{1,2},{2,1},{3,0},{4,7},{5,6},{6,5},{7,4},{8,11},{9,10},{10,... | collective-permute-start | bytes 3342344 | tf_op jit(solution)/shard_map/while/body/eval_jaxpr/cond/branch_3_fun/ppermute | solution.py:208
  168.8 43.6 %collective-permute-start.31 = (bf16[1088,512]{1,0:T(8,128)(2,1)S(1)}, bf16[1088,512]{1,0:T(8,128)(2,1)S(1)}, u32[]{:S(2)}, u32[]{:S(2)}) collective-permute-start(bf16[1088,512]{1,0:T(8,128)(2,1)S(1)} %param.32), channel_id=1, source_target_pairs={{0,64},{1,65},{2,66},{3,67},{4,68},{5,69},{6,70},{7,71},{8,72},{9,... | collective-permute-start | bytes 3342344 | tf_op jit(solution)/shard_map/while/body/eval_jaxpr/cond/branch_32_fun/ppermute | solution.py:208
